TPU v7x, 512 devices: a whole 4x4x16 slice. The times are simulated.
512 devices in a mesh: layer: 4 (over y), row: 16 (over z_lo, core), col: 8 (over z_hi, x).
Axes of the slice: x: 4, y: 4, z: 16 (z_hi: 2, z_lo: 8; z = z_hi * 8 + z_lo), core: 2. Of those that a mesh axis runs over, the one named last changes fastest.
Arguments:
- intermediate: float32 [8192, 65536], P('col', ('layer', 'row')), may hold values from -0.0625 to 0.0625
- amplitudes: float32 [65536, 1024], P(('layer', 'row', 'col')), may hold values from -24 to 24
- occ_irrep: int32 [200], replicated, may hold values from 0 to 7
- vir_irrep: int32 [1800], replicated, may hold values from 0 to 7, as said below
Outputs:
- cycle_term: float32 [1024, 8192], P(('layer', 'row'), 'col')
Inputs may be any that keep to these rules, and one draw needn't show every extreme that they name: `vir_irrep`: in each aligned run of 8 virtual orbitals (0 to 7, 8 to 15, and so on) every irrep 0 to 7 occurs exactly once.
All inputs are finite; a program needn't handle non-finite values.
Results may differ from a plain program's by a relative error of at most 0.0003.
Values sent between devices are 32-bit elements; how exact they have to be, the bound alone decides.
A program may use at most 64 MiB of HBM per device.

v0:
```python
import jax
import jax.numpy as jnp
from jax import lax
from jax.sharding import PartitionSpec as P

OCC = 200


def pair_irreps(offset, count, occ_irrep, vir_irrep):
    indices = offset + jnp.arange(count, dtype=jnp.int32)
    groups = indices // 8
    occupied = jnp.take(occ_irrep, groups % OCC)
    virtual = jnp.take(vir_irrep, 8 * (groups // OCC) + indices % 8)
    return jnp.bitwise_xor(occupied, virtual)


def contract(amp_rows, masked_part):
    return lax.dot_general(
        amp_rows,
        masked_part,
        (((0,), (1,)), ((), ())),
        precision=lax.Precision.HIGHEST,
        preferred_element_type=jnp.float32,
    )


def reduce_pairs(buffer):
    return lax.psum_scatter(buffer, ("layer", "row"), scatter_dimension=1, tiled=True)


def per_device(intermediate, amplitudes, occ_irrep, vir_irrep):
    rows_here = intermediate.shape[0]
    cycle_here = intermediate.shape[1]
    columns = amplitudes.shape[1]
    row_irreps = pair_irreps(lax.axis_index("col") * rows_here, rows_here, occ_irrep, vir_irrep)
    cycle_irreps = pair_irreps(
        lax.axis_index(("layer", "row")) * cycle_here, cycle_here, occ_irrep, vir_irrep
    )
    col_irreps = pair_irreps(0, columns, occ_irrep, vir_irrep)
    masked = jnp.where(
        row_irreps[:, None] == cycle_irreps[None, :], intermediate, jnp.zeros_like(intermediate)
    )
    gathered = lax.all_gather(amplitudes, "col", axis=0, tiled=True)
    partial_sum = contract(gathered, masked)
    partial_sum = jnp.where(
        col_irreps[:, None] == row_irreps[None, :], partial_sum, jnp.zeros_like(partial_sum)
    )
    return reduce_pairs(partial_sum[None, :, :])[0]


def solution(mesh):
    return jax.shard_map(
        per_device,
        mesh=mesh,
        in_specs=(P("col", ("layer", "row")), P(("layer", "row", "col"), None), P(), P()),
        out_specs=P(("layer", "row"), "col"),
        check_vma=False,
    )
```

profile of v0, /device:TPU:1, one launch (start us, length us, event | category | flops | bytes accessed | tf_op | source)
XLA Modules:
  0.0 1065.3 jit_solution(10631101999102809750)
XLA Ops:
  6.5 0.0 copy-start
  6.5 0.0 copy-start.1
  6.5 0.0 all-gather.2.cloned.1.call-start
  6.5 0.7 all-gather.2.cloned.1.call-update
  7.3 0.0 all-reduce.3.cloned.1.call-start
  7.3 6.2 gather_fusion.4
  13.6 0.0 copy-done.1
  13.6 6.9 gather_fusion.2
  20.4 0.0 copy-done
  20.5 6.2 gather_fusion.5
  26.6 6.2 gather_fusion.3
  32.8 5.6 copy.9
  38.3 6.9 gather_fusion
  45.2 6.2 gather_fusion.1
  51.5 143.0 %all-gather.2.cloned.1.call-done = f32[1024,1024]{1,0:T(8,128)} async-done(((f32[128,1024]{1,0:T(8,128)}), f32[1024,1024]{1,0:T(8,128)}) %all-gather.2.cloned.1.call-update) | async-done | bytes 4194320 | tf_op jit(solution)/shard_map/all_gather | solution.py:43
  194.5 18.5 %fusion = f32[1,1024,1024]{1,2,0:T(8,128)} fusion(f32[1024,1024]{1,0:T(8,128)} %all-gather.2.cloned.1.call-done, f32[1024,1024]{0,1:T(8,128)} %copy.9, s32[1024]{0:T(1024)S(1)} %select_xor_fusion.1, s32[1024]{0:T(1024)S(1)} %select_xor_fusion.2, s32[1024]{0:T(1024)S(1)} %select_xor_fusion), kind=kOutput, calls=%fused_computation.7 | convolution fusion | flops 12889096192 | bytes 12595200 | tf_op jit(solution)/shard_map/dot_general | solution.py:18
  213.0 11.0 %copy.10 = f32[1,1024,1024]{2,0,1:T(1,128)} copy(f32[1,1024,1024]{1,2,0:T(8,128)} %fusion) | data formatting | bytes 8388608 | tf_op jit(solution)/shard_map/broadcast_in_dim | solution.py:48
  224.0 0.0 all-reduce.3.cloned.1.call-update
  224.0 1.3 dynamic-slice
  225.9 831.0 %all-reduce.3.cloned.1.call-done = f32[1,1024,1024]{2,0,1:T(1,128)} async-done(((f32[1,1024,1024]{2,0,1:T(1,128)}), f32[1,1024,1024]{2,0,1:T(1,128)}) %all-reduce.3.cloned.1.call-update) | async-done | bytes 4194320
  1057.0 0.8 constant_dynamic-slice_fusion
  1057.8 0.6 copy.13
  (7 shorter events, 0.2 us)
Async XLA Ops:
  6.5 13.9 %copy-start = (s32[1800]{0:T(1024)S(1)}, s32[1800]{0:T(1024)}, u32[]{:S(2)}) copy-start(s32[1800]{0:T(1024)} %param.11) | copy-start | bytes 21604
  6.5 7.0 copy-start.1
  6.5 188.0 %all-gather.2.cloned.1.call-start = ((), (), s32[]{:S(2)}) async-start(), calls=%async_computation | async-start | bytes 4718592 | tf_op jit(solution)/shard_map/all_gather | solution.py:43
  7.3 1049.7 %all-reduce.3.cloned.1.call-start = ((), (), s32[]{:S(2)}) async-start(), calls=%async_computation.1 | async-start | bytes 8388608
Sparse Core Ops, SparseCore 0:
  10.6 183.9 all-gather.1
  224.1 832.8 all-reduce.2
where the time goes:
time: 1070 us
  waiting for transfers between devices  975 us (91%)
  local copies, waits for them, and re-layouts  57.6 us (5%)
  matrix products  18.5 us (2%)
  between operations  14.1 us (1%)
    unnamed x3, waiting for transfers between devices  832 us
    all_gather x1, waiting for transfers between devices, per_device(): gathered = lax.all_gather(amplitudes, 'col', axis=0, tiled=True)  143 us
  transfers between devices with their start and end apart: 2, of which 2 were waited for; matrix products, arithmetic and copies ran while one was open for 4% of the time, Pallas kernels for 0%

commit v1 on v0

v1 whole, which is shorter than its diff:
```python
import jax
import jax.numpy as jnp
from jax import lax
from jax.experimental import pallas as pl
from jax.experimental.pallas import tpu as pltpu
from jax.sharding import PartitionSpec as P

MESH = pl.DeviceIdType.MESH
OCC = 200
IRREPS = 8
LANES = 128
W_CHUNKS = 8


def take_lanes(values, index):
    return jnp.take_along_axis(values, index, axis=1)


def take_rows(values, index):
    return jnp.take_along_axis(values, index, axis=0)


def run_tables(first, offset, occ_low, occ_high, vir_ref, sub):
    virtual = first // OCC
    orbital = first % OCC + offset
    wraps = orbital >= OCC
    orbital = jnp.where(wraps, orbital - OCC, orbital)
    low = take_lanes(occ_low, orbital & (LANES - 1))
    high = take_lanes(occ_high, orbital & (LANES - 1))
    occupied = jnp.where(orbital < LANES, low, high)
    irrep = jnp.zeros_like(sub)
    place = jnp.zeros_like(sub)
    for s in range(IRREPS):
        here = vir_ref[IRREPS * virtual + s]
        after = vir_ref[IRREPS * (virtual + 1) + s]
        value = occupied ^ jnp.where(wraps, after, here)
        irrep = jnp.where(sub == s, value, irrep)
        place = jnp.where(value == sub, s, place)
    return irrep, place


def split(values):
    high = values.astype(jnp.bfloat16)
    low = (values - high.astype(jnp.float32)).astype(jnp.bfloat16)
    return high, low


def kernel(
    w_hbm, a_hbm, occ_ref, vir_ref, out_ref,
    w_raw, a_raw, a_all, w_c, part, core_in, y_out, y_in, z_out, z_in,
    load_sem, col_send, col_recv, red_send, red_recv,
):
    layer, row, col = lax.axis_index("layer"), lax.axis_index("row"), lax.axis_index("col")
    core, z_lo = row % 2, row // 2
    z_hi, x = col // 4, col % 4

    def at(layer_=layer, z_lo_=z_lo, core_=core, col_=col):
        return (layer_, z_lo_ * 2 + core_, col_)

    far_col = (1 - z_hi) * 4 + x
    far = at(col_=far_col)
    x_cols = [z_hi * 4 + (x + k) % 4 for k in range(1, 4)]
    x_peers = [at(col_=c) for c in x_cols]
    y_peers = [at(layer_=(layer + k) % 4) for k in range(1, 4)]
    z_peers = [at(z_lo_=(z_lo + k) % 8) for k in range(1, 8)]
    core_peer = at(core_=1 - core)
    peers = [far, core_peer] + x_peers + y_peers + z_peers

    barrier = pltpu.get_barrier_semaphore()
    for peer in peers:
        pl.semaphore_signal(barrier, inc=1, device_id=peer, device_id_type=MESH)

    a_load = pltpu.make_async_copy(a_hbm, a_raw, load_sem.at[W_CHUNKS])
    a_load.start()
    chunk_rows = w_raw.shape[0] // W_CHUNKS
    w_loads = [
        pltpu.make_async_copy(
            w_hbm.at[pl.ds(n * chunk_rows, chunk_rows)], w_raw.at[pl.ds(n * chunk_rows, chunk_rows)], load_sem.at[n]
        )
        for n in range(W_CHUNKS)
    ]
    for load in w_loads:
        load.start()

    shape = (IRREPS, LANES)
    sub = lax.broadcasted_iota(jnp.int32, shape, 0)
    lane = lax.broadcasted_iota(jnp.int32, shape, 1)
    occ_low = jnp.broadcast_to(occ_ref[0:1, :], shape)
    occ_high = jnp.broadcast_to(occ_ref[1:2, :], shape)
    run_of = ((lane >> 4) & 3) * 32 + ((lane >> 1) & 7) * 4 + (lane >> 6) * 2 + (lane & 1)
    n_irrep, n_place = run_tables(0, run_of, occ_low, occ_high, vir_ref, sub)
    p_irrep, p_place = run_tables((layer * 16 + row) * LANES, lane, occ_low, occ_high, vir_ref, sub)
    m_irrep, m_place = run_tables(col * LANES, lane, occ_low, occ_high, vir_ref, sub)

    def compact(raw_ref, first_row, irrep, place, run, lane_index, block):
        which = jnp.full(shape, run, jnp.int32)
        index = take_rows(lane_index, take_lanes(irrep, which))
        total = jnp.zeros(shape, jnp.float32)
        for k in range(IRREPS):
            values = raw_ref[pl.ds(first_row, IRREPS), pl.ds(k * LANES, LANES)]
            total = jnp.where(block == k, take_lanes(values, index), total)
        return take_rows(total, take_lanes(place, which))

    a_load.wait()
    n_index, n_block = 8 * (run_of & 15) + n_place, run_of >> 4

    def compact_a(j, _):
        rows = pl.multiple_of(j * IRREPS, IRREPS)
        a_all[pl.ds(pl.multiple_of(col * LANES + rows, IRREPS), IRREPS), :] = compact(
            a_raw, rows, p_irrep, p_place, 16 * col + j, n_index, n_block
        )
        return 0

    lax.fori_loop(0, 16, compact_a, 0, unroll=4)

    p_index, p_block = 8 * (lane & 15) + p_place, lane >> 4

    def compact_w(i, _):
        rows = pl.multiple_of(i * IRREPS, IRREPS)
        w_c[pl.ds(rows, IRREPS), :] = compact(w_raw, rows, m_irrep, m_place, i, p_index, p_block)
        return 0

    for n in range(W_CHUNKS):
        w_loads[n].wait()
        runs = LANES // W_CHUNKS
        lax.fori_loop(n * runs, (n + 1) * runs, compact_w, 0, unroll=4)

    pl.semaphore_wait(barrier, len(peers))

    def block(c):
        return a_all.at[pl.ds(pl.multiple_of(c * LANES, LANES), LANES)]

    def col_copy(c, n, peer):
        return pltpu.make_async_remote_copy(
            src_ref=block(c), dst_ref=block(c), send_sem=col_send.at[n], recv_sem=col_recv.at[n],
            device_id=peer, device_id_type=MESH,
        )

    sends = [col_copy(col, 0, far)] + [col_copy(col, 1 + k, x_peers[k]) for k in range(3)]
    for copy in sends:
        copy.start()
    col_copy(far_col, 0, far).wait_recv()
    passes = [col_copy(far_col, 4 + k, x_peers[k]) for k in range(3)]
    for copy in passes:
        copy.start()
    for k in range(3):
        source = (x + 3 - k) % 4
        col_copy(z_hi * 4 + source, 1 + k, x_peers[k]).wait_recv()
        col_copy((1 - z_hi) * 4 + source, 4 + k, x_peers[k]).wait_recv()

    for g in range(IRREPS):
        a_high, a_low = split(a_all[pl.ds(g, LANES, stride=IRREPS), :].T)
        w_high, w_low = split(w_c[pl.ds(g, LANES, stride=IRREPS), :])

        def product(left, right):
            return lax.dot_general(left, right, (((1,), (1,)), ((), ())), preferred_element_type=jnp.float32)

        total = product(a_low, w_high) + product(a_high, w_low) + product(a_high, w_high)
        part[0, g] = total[:64]
        part[1, g] = total[64:]

    def red_copy(source, target, n, peer):
        return pltpu.make_async_remote_copy(
            src_ref=source, dst_ref=target, send_sem=red_send.at[n], recv_sem=red_recv.at[n],
            device_id=peer, device_id_type=MESH,
        )

    copy = red_copy(part.at[1 - core], core_in, 0, core_peer)
    copy.start()
    sends.append(copy)
    copy.wait_recv()
    for g in range(IRREPS):
        total = part[core, g] + core_in[g]
        for k in range(4):
            y_out[k, g] = total[16 * k : 16 * k + 16]

    y_copies = [red_copy(y_out.at[(layer + k) % 4], y_in.at[k - 1], k, y_peers[k - 1]) for k in range(1, 4)]
    for copy in y_copies:
        copy.start()
    for copy in y_copies:
        copy.wait_recv()
    for g in range(IRREPS):
        total = y_out[layer, g] + y_in[0, g] + y_in[1, g] + y_in[2, g]
        z_out[pl.ds(g, 16, stride=IRREPS), :] = total

    def z_rows(z):
        return pl.ds(pl.multiple_of(z * 16, 16), 16)

    z_copies = [red_copy(z_out.at[z_rows((z_lo + k) % 8)], z_in.at[k - 1], 3 + k, z_peers[k - 1]) for k in range(1, 8)]
    for copy in z_copies:
        copy.start()
    for copy in z_copies:
        copy.wait_recv()
    total = z_out[z_rows(z_lo), :]
    for k in range(7):
        total = total + z_in[k]

    first_lane = core * 64 + layer * 16 + z_lo * 2
    for e in range(2):
        order = take_lanes(n_irrep, jnp.full(shape, first_lane + e, jnp.int32))
        for k in range(IRREPS):
            spread = 16 * k + (lane >> 3)
            kept = take_lanes(m_place, spread) == (lane & 7)
            values = jnp.where(kept, take_lanes(total[8 * e : 8 * e + 8], spread), 0.0)
            out_ref[8 * e : 8 * e + 8, k * LANES : (k + 1) * LANES] = take_rows(values, order)

    for copy in sends + passes + y_copies + z_copies:
        copy.wait_send()


def per_device(intermediate, amplitudes, occ_irrep, vir_irrep):
    occupied = jnp.pad(occ_irrep, (0, 2 * LANES - OCC)).reshape(2, LANES)
    vmem = pltpu.VMEM
    f32 = jnp.float32
    return pl.pallas_call(
        kernel,
        out_shape=jax.ShapeDtypeStruct((16, 1024), f32),
        in_specs=[
            pl.BlockSpec(memory_space=pl.ANY),
            pl.BlockSpec(memory_space=pl.ANY),
            pl.BlockSpec(memory_space=vmem),
            pl.BlockSpec(memory_space=pltpu.SMEM),
        ],
        out_specs=pl.BlockSpec(memory_space=vmem),
        scratch_shapes=[
            vmem((1024, 1024), f32),
            vmem((128, 1024), f32),
            vmem((1024, LANES), f32),
            vmem((1024, LANES), f32),
            vmem((2, IRREPS, 64, LANES), f32),
            vmem((IRREPS, 64, LANES), f32),
            vmem((4, IRREPS, 16, LANES), f32),
            vmem((3, IRREPS, 16, LANES), f32),
            vmem((LANES, LANES), f32),
            vmem((7, 16, LANES), f32),
            pltpu.SemaphoreType.DMA((W_CHUNKS + 1,)),
            pltpu.SemaphoreType.DMA((7,)),
            pltpu.SemaphoreType.DMA((7,)),
            pltpu.SemaphoreType.DMA((11,)),
            pltpu.SemaphoreType.DMA((11,)),
        ],
        compiler_params=pltpu.CompilerParams(
            collective_id=0, has_side_effects=True, vmem_limit_bytes=60 * 1024 * 1024
        ),
        name="cycle_contraction",
    )(intermediate, amplitudes, occupied, vir_irrep)


def solution(mesh):
    return jax.shard_map(
        per_device,
        mesh=mesh,
        in_specs=(P("col", ("layer", "row")), P(("layer", "row", "col"), None), P(), P()),
        out_specs=P(("layer", "row"), "col"),
        check_vma=False,
    )
```

time: 1070 us -> 54.2 us (0.05)
  waiting for transfers between devices: 975 us -> 0 us
  local copies, waits for them, and re-layouts: 57.6 us -> 2.72 us
  Pallas kernels: 0 us -> 51.2 us
  matrix products: 18.5 us -> 0 us
  between operations: 14.1 us -> 0.01 us
    unnamed x3 -> x0, waiting for transfers between devices: 832 us -> none
    all_gather x1 -> x0, waiting for transfers between devices: 143 us -> none  [per_device(): gathered = lax.all_gather(amplitudes, 'col', axis=0, tiled=True)]
    pallas_call x0 -> x1, Pallas kernels: none -> 51.2 us  [per_device(): pl.pallas_call(kernel, out_shape=jax.ShapeDtypeStruct((16, 1024), f32), i...]
    gather x6 -> x0, local copies, waits for them, and re-layouts: 38.4 us -> none  [the longest x3 19.9 us: pair_irreps(): occupied = jnp.take(occ_irrep, groups % OCC)]
    dot_general x1 -> x0, matrix products: 18.5 us -> none  [contract(): lax.dot_general(amp_rows, masked_part, (((0,), (1,)), ((), ())), precisio...]
    broadcast_in_dim x1 -> x0, local copies, waits for them, and re-layouts: 11 us -> none  [per_device(): return reduce_pairs(partial_sum[None, :, :])[0]]
  transfers between devices with their start and end apart: 2 -> 0, of which waited for: 2 -> 0; matrix products, arithmetic and copies ran while one was open for 4% -> 0% of each run, Pallas kernels for 0% -> 0%
where the time goes in v1:
time: 54.2 us; the launch traced here: 53.9 us
  Pallas kernels  51.2 us (94%)
  local copies, waits for them, and re-layouts  2.72 us (5%)
    pallas_call x1, Pallas kernels, per_device(): pl.pallas_call(kernel, out_shape=jax.ShapeDtypeStruct((16, 1024), f32), i...  51.2 us
    unnamed x1, local copies, waits for them, and re-layouts  1.47 us
    reshape x1, local copies, waits for them, and re-layouts, per_device(): occupied = jnp.pad(occ_irrep, (0, 2 * LANES - OCC)).reshape(2, LANES)  1.24 us

profile of v1, /device:TPU:1, one launch (start us, length us, event | category | flops | bytes accessed | tf_op | source)
XLA Modules:
  0.0 53.9 jit_solution(15899501395053731002)
XLA Ops:
  0.0 1.2 %pad_bitcast_fusion.occ_ref = s32[2,128]{1,0:T(2,128)} fusion(s32[200]{0:T(256)} %param.6), kind=kLoop, calls=%fused_computation | loop fusion | bytes 1824 | tf_op jit(solution)/shard_map/reshape | solution.py:212
  1.2 51.2 %cycle_contraction.1 = f32[16,1024]{1,0:T(8,128)} custom-call(f32[1024,1024]{1,0:T(8,128)} %w_hbm.1, f32[128,1024]{1,0:T(8,128)} %a_hbm.1, s32[2,128]{1,0:T(2,128)} %pad_bitcast_fusion.occ_ref, s32[1800]{0:T(1024)} %vir_ref.1), custom_call_target="tpu_custom_call" | custom-call | tf_op jit(solution)/shard_map/cycle_contraction/pallas_call | solution.py:215
  52.5 1.5 %copy.6 = f32[16,1024]{1,0:T(8,128)} copy(f32[16,1024]{1,0:T(8,128)} %cycle_contraction.1) | data formatting | bytes 131072

commit v2 on v1

--- a/solution.py
+++ b/solution.py
@@ -10,6 +10,7 @@
 IRREPS = 8
 LANES = 128
 W_CHUNKS = 8
+FAR_CHUNKS = 2
 
 
 def take_lanes(values, index):
@@ -25,8 +26,8 @@
     orbital = first % OCC + offset
     wraps = orbital >= OCC
     orbital = jnp.where(wraps, orbital - OCC, orbital)
-    low = take_lanes(occ_low, orbital & (LANES - 1))
-    high = take_lanes(occ_high, orbital & (LANES - 1))
+    low = take_lanes(occ_low, jnp.minimum(orbital, LANES - 1))
+    high = take_lanes(occ_high, jnp.maximum(orbital - (OCC - LANES), 0))
     occupied = jnp.where(orbital < LANES, low, high)
     irrep = jnp.zeros_like(sub)
     place = jnp.zeros_like(sub)
@@ -48,7 +49,7 @@
 def kernel(
     w_hbm, a_hbm, occ_ref, vir_ref, out_ref,
     w_raw, a_raw, a_all, w_c, part, core_in, y_out, y_in, z_out, z_in,
-    load_sem, col_send, col_recv, red_send, red_recv,
+    load_sem, col_send, col_recv, red_send, red_recv, known,
 ):
     layer, row, col = lax.axis_index("layer"), lax.axis_index("row"), lax.axis_index("col")
     core, z_lo = row % 2, row // 2
@@ -57,36 +58,35 @@
     def at(layer_=layer, z_lo_=z_lo, core_=core, col_=col):
         return (layer_, z_lo_ * 2 + core_, col_)
 
+    def signal(semaphore, peer):
+        pl.semaphore_signal(semaphore, inc=1, device_id=peer, device_id_type=MESH)
+
     far_col = (1 - z_hi) * 4 + x
-    far = at(col_=far_col)
-    x_cols = [z_hi * 4 + (x + k) % 4 for k in range(1, 4)]
-    x_peers = [at(col_=c) for c in x_cols]
+    far, middle = at(col_=far_col), at(z_lo_=z_lo + 4 - 8 * (z_lo // 4))
+    x_peers = [at(col_=z_hi * 4 + (x + k) % 4) for k in range(1, 4)]
     y_peers = [at(layer_=(layer + k) % 4) for k in range(1, 4)]
     z_peers = [at(z_lo_=(z_lo + k) % 8) for k in range(1, 8)]
     core_peer = at(core_=1 - core)
-    peers = [far, core_peer] + x_peers + y_peers + z_peers
+    z_near = [at(z_lo_=z_lo + 1 - 2 * (z_lo % 2)), at(z_lo_=z_lo + 2 - 4 * (z_lo // 2 % 2)), middle]
+    near = z_near + [core_peer, far] + x_peers + y_peers
 
     barrier = pltpu.get_barrier_semaphore()
-    for peer in peers:
-        pl.semaphore_signal(barrier, inc=1, device_id=peer, device_id_type=MESH)
+    for peer in near:
+        signal(barrier, peer)
 
     a_load = pltpu.make_async_copy(a_hbm, a_raw, load_sem.at[W_CHUNKS])
     a_load.start()
     chunk_rows = w_raw.shape[0] // W_CHUNKS
-    w_loads = [
-        pltpu.make_async_copy(
-            w_hbm.at[pl.ds(n * chunk_rows, chunk_rows)], w_raw.at[pl.ds(n * chunk_rows, chunk_rows)], load_sem.at[n]
-        )
-        for n in range(W_CHUNKS)
-    ]
-    for load in w_loads:
-        load.start()
+
+    def w_load(n):
+        rows = pl.ds(pl.multiple_of(n * chunk_rows, chunk_rows), chunk_rows)
+        return pltpu.make_async_copy(w_hbm.at[rows], w_raw.at[rows], load_sem.at[n])
 
     shape = (IRREPS, LANES)
     sub = lax.broadcasted_iota(jnp.int32, shape, 0)
     lane = lax.broadcasted_iota(jnp.int32, shape, 1)
-    occ_low = jnp.broadcast_to(occ_ref[0:1, :], shape)
-    occ_high = jnp.broadcast_to(occ_ref[1:2, :], shape)
+    occ_low = jnp.broadcast_to(occ_ref[pl.ds(0, LANES)][None, :], shape)
+    occ_high = jnp.broadcast_to(occ_ref[pl.ds(OCC - LANES, LANES)][None, :], shape)
     run_of = ((lane >> 4) & 3) * 32 + ((lane >> 1) & 7) * 4 + (lane >> 6) * 2 + (lane & 1)
     n_irrep, n_place = run_tables(0, run_of, occ_low, occ_high, vir_ref, sub)
     p_irrep, p_place = run_tables((layer * 16 + row) * LANES, lane, occ_low, occ_high, vir_ref, sub)
@@ -102,6 +102,8 @@
         return take_rows(total, take_lanes(place, which))
 
     a_load.wait()
+    for n in range(W_CHUNKS):
+        w_load(n).start()
     n_index, n_block = 8 * (run_of & 15) + n_place, run_of >> 4
 
     def compact_a(j, _):
@@ -111,7 +113,32 @@
         )
         return 0
 
-    lax.fori_loop(0, 16, compact_a, 0, unroll=4)
+    lax.fori_loop(0, 16, compact_a, 0, unroll=8)
+
+    pl.semaphore_wait(barrier, len(near))
+
+    far_rows = LANES // FAR_CHUNKS
+    x_at, far_at, pass_at = 0, 3, 3 + FAR_CHUNKS
+
+    def block(ref, c, n=None):
+        start, rows = (0, LANES) if n is None else (n * far_rows, far_rows)
+        return ref.at[pl.ds(pl.multiple_of(c * LANES + start, far_rows), rows)]
+
+    def col_copy(source, target, n, peer):
+        return pltpu.make_async_remote_copy(
+            src_ref=source, dst_ref=target, send_sem=col_send.at[n], recv_sem=col_recv.at[n],
+            device_id=peer, device_id_type=MESH,
+        )
+
+    to_far = [col_copy(block(a_all, col, n), block(a_all, col, n), far_at + n, far) for n in range(FAR_CHUNKS)]
+    own_x = [col_copy(block(a_all, col), block(a_all, col), x_at + k, x_peers[k]) for k in range(3)]
+
+    for copy in to_far:
+        copy.start()
+    for copy in own_x:
+        copy.start()
+    for peer in z_near:
+        signal(known.at[0], peer)
 
     p_index, p_block = 8 * (lane & 15) + p_place, lane >> 4
 
@@ -120,35 +147,37 @@
         w_c[pl.ds(rows, IRREPS), :] = compact(w_raw, rows, m_irrep, m_place, i, p_index, p_block)
         return 0
 
-    for n in range(W_CHUNKS):
-        w_loads[n].wait()
+    def compact_chunk(n, _):
+        w_load(n).wait()
         runs = LANES // W_CHUNKS
-        lax.fori_loop(n * runs, (n + 1) * runs, compact_w, 0, unroll=4)
-
-    pl.semaphore_wait(barrier, len(peers))
-
-    def block(c):
-        return a_all.at[pl.ds(pl.multiple_of(c * LANES, LANES), LANES)]
-
-    def col_copy(c, n, peer):
-        return pltpu.make_async_remote_copy(
-            src_ref=block(c), dst_ref=block(c), send_sem=col_send.at[n], recv_sem=col_recv.at[n],
-            device_id=peer, device_id_type=MESH,
-        )
-
-    sends = [col_copy(col, 0, far)] + [col_copy(col, 1 + k, x_peers[k]) for k in range(3)]
-    for copy in sends:
-        copy.start()
-    col_copy(far_col, 0, far).wait_recv()
-    passes = [col_copy(far_col, 4 + k, x_peers[k]) for k in range(3)]
-    for copy in passes:
-        copy.start()
+        for i in range(runs):
+            compact_w(n * runs + i, 0)
+        return 0
+
+    lax.fori_loop(0, W_CHUNKS, compact_chunk, 0)
+
+    pl.semaphore_wait(known.at[0], len(z_near))
+    for peer in z_near:
+        signal(known.at[1], peer)
+
+    passes = []
+    for n in range(FAR_CHUNKS):
+        col_copy(block(a_all, far_col, n), block(a_all, far_col, n), far_at + n, far).wait_recv()
+        for k in range(3):
+            copy = col_copy(
+                block(a_all, far_col, n), block(a_all, far_col, n), pass_at + 3 * n + k, x_peers[k]
+            )
+            copy.start()
+            passes.append(copy)
     for k in range(3):
         source = (x + 3 - k) % 4
-        col_copy(z_hi * 4 + source, 1 + k, x_peers[k]).wait_recv()
-        col_copy((1 - z_hi) * 4 + source, 4 + k, x_peers[k]).wait_recv()
-
-    for g in range(IRREPS):
+        mine = block(a_all, z_hi * 4 + source)
+        col_copy(mine, mine, x_at + k, x_peers[k]).wait_recv()
+        for n in range(FAR_CHUNKS):
+            passed = block(a_all, (1 - z_hi) * 4 + source, n)
+            col_copy(passed, passed, pass_at + 3 * n + k, x_peers[k]).wait_recv()
+
+    def multiply(g, _):
         a_high, a_low = split(a_all[pl.ds(g, LANES, stride=IRREPS), :].T)
         w_high, w_low = split(w_c[pl.ds(g, LANES, stride=IRREPS), :])
 
@@ -158,6 +187,9 @@
         total = product(a_low, w_high) + product(a_high, w_low) + product(a_high, w_high)
         part[0, g] = total[:64]
         part[1, g] = total[64:]
+        return 0
+
+    lax.fori_loop(0, IRREPS, multiply, 0, unroll=2)
 
     def red_copy(source, target, n, peer):
         return pltpu.make_async_remote_copy(
@@ -165,14 +197,16 @@
             device_id=peer, device_id_type=MESH,
         )
 
-    copy = red_copy(part.at[1 - core], core_in, 0, core_peer)
-    copy.start()
-    sends.append(copy)
-    copy.wait_recv()
-    for g in range(IRREPS):
+    core_copy = red_copy(part.at[1 - core], core_in, 0, core_peer)
+    core_copy.start()
+    core_copy.wait_recv()
+    def add_core(g, _):
         total = part[core, g] + core_in[g]
         for k in range(4):
             y_out[k, g] = total[16 * k : 16 * k + 16]
+        return 0
+
+    lax.fori_loop(0, IRREPS, add_core, 0)
 
     y_copies = [red_copy(y_out.at[(layer + k) % 4], y_in.at[k - 1], k, y_peers[k - 1]) for k in range(1, 4)]
     for copy in y_copies:
@@ -182,6 +216,8 @@
     for g in range(IRREPS):
         total = y_out[layer, g] + y_in[0, g] + y_in[1, g] + y_in[2, g]
         z_out[pl.ds(g, 16, stride=IRREPS), :] = total
+
+    pl.semaphore_wait(known.at[1], len(z_near))
 
     def z_rows(z):
         return pl.ds(pl.multiple_of(z * 16, 16), 16)
@@ -204,12 +240,11 @@
             values = jnp.where(kept, take_lanes(total[8 * e : 8 * e + 8], spread), 0.0)
             out_ref[8 * e : 8 * e + 8, k * LANES : (k + 1) * LANES] = take_rows(values, order)
 
-    for copy in sends + passes + y_copies + z_copies:
+    for copy in to_far + own_x + passes + [core_copy] + y_copies + z_copies:
         copy.wait_send()
 
 
 def per_device(intermediate, amplitudes, occ_irrep, vir_irrep):
-    occupied = jnp.pad(occ_irrep, (0, 2 * LANES - OCC)).reshape(2, LANES)
     vmem = pltpu.VMEM
     f32 = jnp.float32
     return pl.pallas_call(
@@ -234,16 +269,17 @@
             vmem((LANES, LANES), f32),
             vmem((7, 16, LANES), f32),
             pltpu.SemaphoreType.DMA((W_CHUNKS + 1,)),
-            pltpu.SemaphoreType.DMA((7,)),
-            pltpu.SemaphoreType.DMA((7,)),
+            pltpu.SemaphoreType.DMA((3 + 4 * FAR_CHUNKS,)),
+            pltpu.SemaphoreType.DMA((3 + 4 * FAR_CHUNKS,)),
             pltpu.SemaphoreType.DMA((11,)),
             pltpu.SemaphoreType.DMA((11,)),
+            pltpu.SemaphoreType.REGULAR((2,)),
         ],
         compiler_params=pltpu.CompilerParams(
             collective_id=0, has_side_effects=True, vmem_limit_bytes=60 * 1024 * 1024
         ),
         name="cycle_contraction",
-    )(intermediate, amplitudes, occupied, vir_irrep)
+    )(intermediate, amplitudes, occ_irrep, vir_irrep)
 
 
 def solution(mesh):

time: 54.2 us -> 47.9 us (0.88)
  Pallas kernels: 51.2 us -> 46.1 us
  local copies, waits for them, and re-layouts: 2.72 us -> 1.47 us
    pallas_call x1, Pallas kernels: 51.2 us -> 46.1 us  [per_device(): pl.pallas_call(kernel, out_shape=jax.ShapeDtypeStruct((16, 1024), f32), i...]
    reshape x1 -> x0, local copies, waits for them, and re-layouts: 1.24 us -> none  [per_device(): occupied = jnp.pad(occ_irrep, (0, 2 * LANES - OCC)).reshape(2, LANES)]
where the time goes in v2:
time: 47.9 us; the launch traced here: 47.6 us
  Pallas kernels  46.1 us (96%)
  local copies, waits for them, and re-layouts  1.47 us (3%)
    pallas_call x1, Pallas kernels, per_device(): pl.pallas_call(kernel, out_shape=jax.ShapeDtypeStruct((16, 1024), f32), i...  46.1 us
    unnamed x1, local copies, waits for them, and re-layouts  1.47 us

profile of v2, /device:TPU:1, one launch (start us, length us, event | category | flops | bytes accessed | tf_op | source)
XLA Modules:
  0.0 47.6 jit_solution(1542933018947351322)
XLA Ops:
  0.0 46.1 %cycle_contraction.1 = f32[16,1024]{1,0:T(8,128)} custom-call(f32[1024,1024]{1,0:T(8,128)} %w_hbm.1, f32[128,1024]{1,0:T(8,128)} %a_hbm.1, s32[200]{0:T(256)} %occ_ref.1, s32[1800]{0:T(1024)} %vir_ref.1), custom_call_target="tpu_custom_call" | custom-call | tf_op jit(solution)/shard_map/cycle_contraction/pallas_call | solution.py:250
  46.1 1.5 %copy.6 = f32[16,1024]{1,0:T(8,128)} copy(f32[16,1024]{1,0:T(8,128)} %cycle_contraction.1) | data formatting | bytes 131072

commit v3 on v2

--- a/solution.py
+++ b/solution.py
@@ -10,6 +10,7 @@
 IRREPS = 8
 LANES = 128
 W_CHUNKS = 8
+OPPOSITE_FIRST = (1, 0, 2)
 FAR_CHUNKS = 2
 
 
@@ -47,8 +48,8 @@
 
 
 def kernel(
-    w_hbm, a_hbm, occ_ref, vir_ref, out_ref,
-    w_raw, a_raw, a_all, w_c, part, core_in, y_out, y_in, z_out, z_in,
+    w_hbm, a_hbm, occ_hbm, vir_hbm, out_ref,
+    occ_ref, vir_ref, w_raw, a_raw, a_all, w_c, part, core_in, y_out, y_in, z_out, z_in,
     load_sem, col_send, col_recv, red_send, red_recv, known,
 ):
     layer, row, col = lax.axis_index("layer"), lax.axis_index("row"), lax.axis_index("col")
@@ -75,7 +76,10 @@
         signal(barrier, peer)
 
     a_load = pltpu.make_async_copy(a_hbm, a_raw, load_sem.at[W_CHUNKS])
-    a_load.start()
+    occ_load = pltpu.make_async_copy(occ_hbm, occ_ref, load_sem.at[W_CHUNKS + 1])
+    vir_load = pltpu.make_async_copy(vir_hbm, vir_ref, load_sem.at[W_CHUNKS + 2])
+    for load in (vir_load, occ_load, a_load):
+        load.start()
     chunk_rows = w_raw.shape[0] // W_CHUNKS
 
     def w_load(n):
@@ -85,12 +89,13 @@
     shape = (IRREPS, LANES)
     sub = lax.broadcasted_iota(jnp.int32, shape, 0)
     lane = lax.broadcasted_iota(jnp.int32, shape, 1)
+    occ_load.wait()
+    vir_load.wait()
     occ_low = jnp.broadcast_to(occ_ref[pl.ds(0, LANES)][None, :], shape)
     occ_high = jnp.broadcast_to(occ_ref[pl.ds(OCC - LANES, LANES)][None, :], shape)
     run_of = ((lane >> 4) & 3) * 32 + ((lane >> 1) & 7) * 4 + (lane >> 6) * 2 + (lane & 1)
     n_irrep, n_place = run_tables(0, run_of, occ_low, occ_high, vir_ref, sub)
     p_irrep, p_place = run_tables((layer * 16 + row) * LANES, lane, occ_low, occ_high, vir_ref, sub)
-    m_irrep, m_place = run_tables(col * LANES, lane, occ_low, occ_high, vir_ref, sub)
 
     def compact(raw_ref, first_row, irrep, place, run, lane_index, block):
         which = jnp.full(shape, run, jnp.int32)
@@ -135,11 +140,12 @@
 
     for copy in to_far:
         copy.start()
-    for copy in own_x:
-        copy.start()
+    for k in OPPOSITE_FIRST:
+        own_x[k].start()
     for peer in z_near:
         signal(known.at[0], peer)
 
+    m_irrep, m_place = run_tables(col * LANES, lane, occ_low, occ_high, vir_ref, sub)
     p_index, p_block = 8 * (lane & 15) + p_place, lane >> 4
 
     def compact_w(i, _):
@@ -163,7 +169,7 @@
     passes = []
     for n in range(FAR_CHUNKS):
         col_copy(block(a_all, far_col, n), block(a_all, far_col, n), far_at + n, far).wait_recv()
-        for k in range(3):
+        for k in OPPOSITE_FIRST:
             copy = col_copy(
                 block(a_all, far_col, n), block(a_all, far_col, n), pass_at + 3 * n + k, x_peers[k]
             )
@@ -177,19 +183,28 @@
             passed = block(a_all, (1 - z_hi) * 4 + source, n)
             col_copy(passed, passed, pass_at + 3 * n + k, x_peers[k]).wait_recv()
 
-    def multiply(g, _):
-        a_high, a_low = split(a_all[pl.ds(g, LANES, stride=IRREPS), :].T)
+    def product(left, right):
+        return lax.dot_general(left, right, (((1,), (1,)), ((), ())), preferred_element_type=jnp.float32)
+
+    def multiply(left, g):
+        high, low = split(left)
         w_high, w_low = split(w_c[pl.ds(g, LANES, stride=IRREPS), :])
-
-        def product(left, right):
-            return lax.dot_general(left, right, (((1,), (1,)), ((), ())), preferred_element_type=jnp.float32)
-
-        total = product(a_low, w_high) + product(a_high, w_low) + product(a_high, w_high)
-        part[0, g] = total[:64]
-        part[1, g] = total[64:]
-        return 0
-
-    lax.fori_loop(0, IRREPS, multiply, 0, unroll=2)
+        return product(low, w_high) + product(high, w_low) + product(high, w_high)
+
+    def multiply_other(g, _):
+        left = a_all[pl.ds(g, LANES, stride=IRREPS), :].T
+        part[0, g] = multiply(jnp.where(core == 0, left[64:], left[:64]), g)
+        part[1, g] = jnp.where(core == 0, left[:64], left[64:])
+        return 0
+
+    def multiply_own(g, _):
+        part[1, g] = multiply(part[1, g], g)
+        return 0
+
+    half = IRREPS // 2
+
+    def group(q):
+        return pl.ds(q * half, half)
 
     def red_copy(source, target, n, peer):
         return pltpu.make_async_remote_copy(
@@ -197,50 +212,72 @@
             device_id=peer, device_id_type=MESH,
         )
 
-    core_copy = red_copy(part.at[1 - core], core_in, 0, core_peer)
-    core_copy.start()
-    core_copy.wait_recv()
+    core_copies = [red_copy(part.at[0, group(q)], core_in.at[group(q)], 11 * q, core_peer) for q in range(2)]
+    for q in range(2):
+        lax.fori_loop(q * half, (q + 1) * half, multiply_other, 0, unroll=2)
+        core_copies[q].start()
+    lax.fori_loop(0, IRREPS, multiply_own, 0, unroll=2)
+
     def add_core(g, _):
-        total = part[core, g] + core_in[g]
+        total = part[1, g] + core_in[g]
         for k in range(4):
             y_out[k, g] = total[16 * k : 16 * k + 16]
         return 0
 
-    lax.fori_loop(0, IRREPS, add_core, 0)
-
-    y_copies = [red_copy(y_out.at[(layer + k) % 4], y_in.at[k - 1], k, y_peers[k - 1]) for k in range(1, 4)]
-    for copy in y_copies:
-        copy.start()
-    for copy in y_copies:
-        copy.wait_recv()
-    for g in range(IRREPS):
-        total = y_out[layer, g] + y_in[0, g] + y_in[1, g] + y_in[2, g]
-        z_out[pl.ds(g, 16, stride=IRREPS), :] = total
+    y_copies = [
+        [
+            red_copy(y_out.at[(layer + k) % 4, group(q)], y_in.at[k - 1, group(q)], 11 * q + k, y_peers[k - 1])
+            for k in range(1, 4)
+        ]
+        for q in range(2)
+    ]
+    for q in range(2):
+        core_copies[q].wait_recv()
+        lax.fori_loop(q * half, (q + 1) * half, add_core, 0)
+        for k in OPPOSITE_FIRST:
+            y_copies[q][k].start()
 
     pl.semaphore_wait(known.at[1], len(z_near))
 
     def z_rows(z):
-        return pl.ds(pl.multiple_of(z * 16, 16), 16)
-
-    z_copies = [red_copy(z_out.at[z_rows((z_lo + k) % 8)], z_in.at[k - 1], 3 + k, z_peers[k - 1]) for k in range(1, 8)]
-    for copy in z_copies:
-        copy.start()
-    for copy in z_copies:
-        copy.wait_recv()
-    total = z_out[z_rows(z_lo), :]
-    for k in range(7):
-        total = total + z_in[k]
+        return pl.ds(pl.multiple_of(z * 8, 8), 8)
+
+    z_copies = [
+        [
+            red_copy(z_out.at[q, z_rows((z_lo + k) % 8)], z_in.at[q, k - 1], 11 * q + 3 + k, z_peers[k - 1])
+            for k in range(1, 8)
+        ]
+        for q in range(2)
+    ]
+    for q in range(2):
+        for copy in y_copies[q]:
+            copy.wait_recv()
+        for n in range(half):
+            g = q * half + n
+            total = y_out[layer, g] + y_in[0, g] + y_in[1, g] + y_in[2, g]
+            z_out[q, pl.ds(n, 16, stride=half), :] = total
+        for copy in z_copies[q]:
+            copy.start()
+
+    totals = []
+    for q in range(2):
+        total = z_out[q, z_rows(z_lo), :]
+        for k in range(7):
+            z_copies[q][k].wait_recv()
+            total = total + z_in[q, k]
+        totals.append(total)
 
     first_lane = core * 64 + layer * 16 + z_lo * 2
     for e in range(2):
+        mine = jnp.concatenate([total[half * e : half * e + half] for total in totals], axis=0)
         order = take_lanes(n_irrep, jnp.full(shape, first_lane + e, jnp.int32))
         for k in range(IRREPS):
             spread = 16 * k + (lane >> 3)
             kept = take_lanes(m_place, spread) == (lane & 7)
-            values = jnp.where(kept, take_lanes(total[8 * e : 8 * e + 8], spread), 0.0)
+            values = jnp.where(kept, take_lanes(mine, spread), 0.0)
             out_ref[8 * e : 8 * e + 8, k * LANES : (k + 1) * LANES] = take_rows(values, order)
 
-    for copy in to_far + own_x + passes + [core_copy] + y_copies + z_copies:
+    for copy in to_far + own_x + passes + core_copies + y_copies[0] + y_copies[1] + z_copies[0] + z_copies[1]:
         copy.wait_send()
 
 
@@ -253,11 +290,13 @@
         in_specs=[
             pl.BlockSpec(memory_space=pl.ANY),
             pl.BlockSpec(memory_space=pl.ANY),
-            pl.BlockSpec(memory_space=vmem),
-            pl.BlockSpec(memory_space=pltpu.SMEM),
+            pl.BlockSpec(memory_space=pl.ANY),
+            pl.BlockSpec(memory_space=pl.ANY),
         ],
         out_specs=pl.BlockSpec(memory_space=vmem),
         scratch_shapes=[
+            vmem((200,), jnp.int32),
+            pltpu.SMEM((1800,), jnp.int32),
             vmem((1024, 1024), f32),
             vmem((128, 1024), f32),
             vmem((1024, LANES), f32),
@@ -266,13 +305,13 @@
             vmem((IRREPS, 64, LANES), f32),
             vmem((4, IRREPS, 16, LANES), f32),
             vmem((3, IRREPS, 16, LANES), f32),
-            vmem((LANES, LANES), f32),
-            vmem((7, 16, LANES), f32),
-            pltpu.SemaphoreType.DMA((W_CHUNKS + 1,)),
+            vmem((2, 64, LANES), f32),
+            vmem((2, 7, 8, LANES), f32),
+            pltpu.SemaphoreType.DMA((W_CHUNKS + 3,)),
             pltpu.SemaphoreType.DMA((3 + 4 * FAR_CHUNKS,)),
             pltpu.SemaphoreType.DMA((3 + 4 * FAR_CHUNKS,)),
-            pltpu.SemaphoreType.DMA((11,)),
-            pltpu.SemaphoreType.DMA((11,)),
+            pltpu.SemaphoreType.DMA((22,)),
+            pltpu.SemaphoreType.DMA((22,)),
             pltpu.SemaphoreType.REGULAR((2,)),
         ],
         compiler_params=pltpu.CompilerParams(

time: 47.9 us -> 46 us (0.960)
  Pallas kernels: 46.1 us -> 44.3 us
    pallas_call x1, Pallas kernels: 46.1 us -> 44.3 us  [per_device(): pl.pallas_call(kernel, out_shape=jax.ShapeDtypeStruct((16, 1024), f32), i...]
where the time goes in v3:
time: 46 us; the launch traced here: 45.8 us
  Pallas kernels  44.3 us (96%)
  local copies, waits for them, and re-layouts  1.47 us (3%)
    pallas_call x1, Pallas kernels, per_device(): pl.pallas_call(kernel, out_shape=jax.ShapeDtypeStruct((16, 1024), f32), i...  44.3 us
    unnamed x1, local copies, waits for them, and re-layouts  1.47 us

profile of v3, /device:TPU:1, one launch (start us, length us, event | category | flops | bytes accessed | tf_op | source)
XLA Modules:
  0.0 45.8 jit_solution(2172669527900995990)
XLA Ops:
  0.0 44.3 %cycle_contraction.1 = f32[16,1024]{1,0:T(8,128)} custom-call(f32[1024,1024]{1,0:T(8,128)} %w_hbm.1, f32[128,1024]{1,0:T(8,128)} %a_hbm.1, s32[200]{0:T(256)} %occ_hbm.1, s32[1800]{0:T(1024)} %vir_hbm.1), custom_call_target="tpu_custom_call" | custom-call | tf_op jit(solution)/shard_map/cycle_contraction/pallas_call | solution.py:287
  44.3 1.5 %copy.6 = f32[16,1024]{1,0:T(8,128)} copy(f32[16,1024]{1,0:T(8,128)} %cycle_contraction.1) | data formatting | bytes 131072

commit v4 on v3

--- a/solution.py
+++ b/solution.py
@@ -48,7 +48,7 @@
 
 
 def kernel(
-    w_hbm, a_hbm, occ_hbm, vir_hbm, out_ref,
+    w_hbm, a_hbm, occ_hbm, vir_hbm, sums_ref, order_ref, place_ref,
     occ_ref, vir_ref, w_raw, a_raw, a_all, w_c, part, core_in, y_out, y_in, z_out, z_in,
     load_sem, col_send, col_recv, red_send, red_recv, known,
 ):
@@ -118,7 +118,7 @@
         )
         return 0
 
-    lax.fori_loop(0, 16, compact_a, 0, unroll=8)
+    lax.fori_loop(0, 16, compact_a, 0, unroll=16)
 
     pl.semaphore_wait(barrier, len(near))
 
@@ -259,6 +259,10 @@
         for copy in z_copies[q]:
             copy.start()
 
+    first_lane = core * 64 + layer * 16 + z_lo * 2
+    for e in range(2):
+        order_ref[8 * e : 8 * e + 8, :] = take_lanes(n_irrep, jnp.full(shape, first_lane + e, jnp.int32))
+    place_ref[...] = m_place
     totals = []
     for q in range(2):
         total = z_out[q, z_rows(z_lo), :]
@@ -267,33 +271,41 @@
             total = total + z_in[q, k]
         totals.append(total)
 
-    first_lane = core * 64 + layer * 16 + z_lo * 2
     for e in range(2):
-        mine = jnp.concatenate([total[half * e : half * e + half] for total in totals], axis=0)
-        order = take_lanes(n_irrep, jnp.full(shape, first_lane + e, jnp.int32))
-        for k in range(IRREPS):
-            spread = 16 * k + (lane >> 3)
-            kept = take_lanes(m_place, spread) == (lane & 7)
-            values = jnp.where(kept, take_lanes(mine, spread), 0.0)
-            out_ref[8 * e : 8 * e + 8, k * LANES : (k + 1) * LANES] = take_rows(values, order)
+        mine = [total[half * e : half * e + half] for total in totals]
+        sums_ref[8 * e : 8 * e + 8, :] = jnp.concatenate(mine, axis=0)
 
     for copy in to_far + own_x + passes + core_copies + y_copies[0] + y_copies[1] + z_copies[0] + z_copies[1]:
         copy.wait_send()
+
+
+def expand(sums_ref, order_ref, place_ref, out_ref):
+    lane = lax.broadcasted_iota(jnp.int32, (IRREPS, LANES), 1)
+    for k in range(IRREPS):
+        spread = 16 * k + (lane >> 3)
+        kept = take_lanes(place_ref[...], spread) == (lane & 7)
+        for rows in (slice(0, 8), slice(8, 16)):
+            values = jnp.where(kept, take_lanes(sums_ref[rows, :], spread), 0.0)
+            out_ref[rows, k * LANES : (k + 1) * LANES] = take_rows(values, order_ref[rows, :])
 
 
 def per_device(intermediate, amplitudes, occ_irrep, vir_irrep):
     vmem = pltpu.VMEM
     f32 = jnp.float32
-    return pl.pallas_call(
+    sums, order, place = pl.pallas_call(
         kernel,
-        out_shape=jax.ShapeDtypeStruct((16, 1024), f32),
+        out_shape=[
+            jax.ShapeDtypeStruct((16, LANES), f32),
+            jax.ShapeDtypeStruct((16, LANES), jnp.int32),
+            jax.ShapeDtypeStruct((IRREPS, LANES), jnp.int32),
+        ],
         in_specs=[
             pl.BlockSpec(memory_space=pl.ANY),
             pl.BlockSpec(memory_space=pl.ANY),
             pl.BlockSpec(memory_space=pl.ANY),
             pl.BlockSpec(memory_space=pl.ANY),
         ],
-        out_specs=pl.BlockSpec(memory_space=vmem),
+        out_specs=[pl.BlockSpec(memory_space=vmem)] * 3,
         scratch_shapes=[
             vmem((200,), jnp.int32),
             pltpu.SMEM((1800,), jnp.int32),
@@ -319,6 +331,13 @@
         ),
         name="cycle_contraction",
     )(intermediate, amplitudes, occ_irrep, vir_irrep)
+    return pl.pallas_call(
+        expand,
+        out_shape=jax.ShapeDtypeStruct((16, 1024), f32),
+        in_specs=[pl.BlockSpec(memory_space=vmem)] * 3,
+        out_specs=pl.BlockSpec(memory_space=vmem),
+        name="expand_irreps",
+    )(sums, order, place)
 
 
 def solution(mesh):

time: 46 us -> 45.8 us (level)
  local copies, waits for them, and re-layouts: 1.47 us -> 0 us
  Pallas kernels: 44.3 us -> 45.6 us
    unnamed x1 -> x0, local copies, waits for them, and re-layouts: 1.47 us -> none
    pallas_call x1 -> x2, Pallas kernels: 44.3 us -> 45.6 us  [the longest x1 44.2 us: per_device(): pl.pallas_call(kernel, out_shape=[jax.ShapeDtypeStruct((16, LANES), f32),...]
where the time goes in v4:
time: 45.8 us; the launch traced here: 45.6 us
  Pallas kernels  45.6 us (100%)
    pallas_call x1, Pallas kernels, per_device(): pl.pallas_call(kernel, out_shape=[jax.ShapeDtypeStruct((16, LANES), f32),...  44.2 us
    pallas_call x1, Pallas kernels, per_device(): pl.pallas_call(expand, out_shape=jax.ShapeDtypeStruct((16, 1024), f32), i...  1.48 us

profile of v4, /device:TPU:1, one launch (start us, length us, event | category | flops | bytes accessed | tf_op | source)
XLA Modules:
  0.0 45.6 jit_solution(12165381977657883139)
XLA Ops:
  0.0 44.2 %cycle_contraction.1 = (f32[16,128]{1,0:T(8,128)}, s32[16,128]{1,0:T(8,128)}, s32[8,128]{1,0:T(8,128)}) custom-call(f32[1024,1024]{1,0:T(8,128)} %w_hbm.1, f32[128,1024]{1,0:T(8,128)} %a_hbm.1, s32[200]{0:T(256)} %occ_hbm.1, s32[1800]{0:T(1024)} %vir_hbm.1), custom_call_target="tpu_custom_call" | custom-call | tf_op jit(solution)/shard_map/cycle_contraction/pallas_call | solution.py:295
  44.2 1.5 %expand_irreps.1 = f32[16,1024]{1,0:T(8,128)} custom-call(f32[16,128]{1,0:T(8,128)} %get-tuple-element.8.sums_ref, s32[16,128]{1,0:T(8,128)} %get-tuple-element.9.order_ref, s32[8,128]{1,0:T(8,128)} %get-tuple-element.10.place_ref), custom_call_target="tpu_custom_call" | custom-call | tf_op jit(solution)/shard_map/expand_irreps/pallas_call | solution.py:334

commit v5 on v4

--- a/solution.py
+++ b/solution.py
@@ -11,7 +11,7 @@
 LANES = 128
 W_CHUNKS = 8
 OPPOSITE_FIRST = (1, 0, 2)
-FAR_CHUNKS = 2
+FAR_CHUNKS = 4
 
 
 def take_lanes(values, index):

time: 45.8 us -> 45.9 us (level)
  no operation moved by 1% of the time
where the time goes in v5:
time: 45.9 us; the launch traced here: 45.7 us
  Pallas kernels  45.7 us (100%)
    pallas_call x1, Pallas kernels, per_device(): pl.pallas_call(kernel, out_shape=[jax.ShapeDtypeStruct((16, LANES), f32),...  44.2 us
    pallas_call x1, Pallas kernels, per_device(): pl.pallas_call(expand, out_shape=jax.ShapeDtypeStruct((16, 1024), f32), i...  1.48 us

profile of v5, /device:TPU:1, one launch (start us, length us, event | category | flops | bytes accessed | tf_op | source)
XLA Modules:
  0.0 45.7 jit_solution(15756748717633969228)
XLA Ops:
  0.0 44.2 %cycle_contraction.1 = (f32[16,128]{1,0:T(8,128)}, s32[16,128]{1,0:T(8,128)}, s32[8,128]{1,0:T(8,128)}) custom-call(f32[1024,1024]{1,0:T(8,128)} %w_hbm.1, f32[128,1024]{1,0:T(8,128)} %a_hbm.1, s32[200]{0:T(256)} %occ_hbm.1, s32[1800]{0:T(1024)} %vir_hbm.1), custom_call_target="tpu_custom_call" | custom-call | tf_op jit(solution)/shard_map/cycle_contraction/pallas_call | solution.py:295
  44.2 1.5 %expand_irreps.1 = f32[16,1024]{1,0:T(8,128)} custom-call(f32[16,128]{1,0:T(8,128)} %get-tuple-element.8.sums_ref, s32[16,128]{1,0:T(8,128)} %get-tuple-element.9.order_ref, s32[8,128]{1,0:T(8,128)} %get-tuple-element.10.place_ref), custom_call_target="tpu_custom_call" | custom-call | tf_op jit(solution)/shard_map/expand_irreps/pallas_call | solution.py:334
